TPU v7x, 32 devices: a whole 2x2x4 slice. The times are simulated.
32 devices in a mesh: seq: 4 (over z), video: 8 (over y, x, core).
Axes of the slice: x: 2, y: 2, z: 4, core: 2. Of those that a mesh axis runs over, the one named last changes fastest.
Arguments:
- queries: bfloat16 [8, 512, 3072], P('video', 'seq'), may hold values from -256 to 256
- kv_current: bfloat16 [8, 512, 1024], P('video', 'seq'), may hold values from -6 to 6
- kv_history: bfloat16 [8, 2, 512, 1024], P('video', None, 'seq'), may hold values from -6 to 6
- noisy_latent: float32 [8, 512, 64], P('video', 'seq'), may hold values from -6 to 6
- head_weight: bfloat16 [3072, 64], replicated, may hold values from -0.109375 to 0.109375
- timesteps: int32 [8], P('video'), may hold values from 250 to 1000
- counts: int32 [8], P('video'), may hold values from 0 to 2, as said below
- past_latent: bfloat16 [8, 32, 512], P('video', 'seq'), may hold values from -6 to 6
- tile_lists: int32 [8, 32, 1], P('video', 'seq'), may hold values from 0 to 7; in each aligned block of 8 rows (0 to 7, 8 to 15, ..., all dimensions but the last counted through in order) at most 2 rows name the same one
- conv_in_weight: bfloat16 [432, 256], replicated, may hold values from -0.3125 to 0.3125
- conv_weight: bfloat16 [6912, 256], replicated, may hold values from -0.078125 to 0.078125
- norm_gain: float32 [256], replicated, may hold values from 0.1 to 1.9
Outputs:
- next_latent: bfloat16 [8, 512, 64], P('video', 'seq')
- decoded: bfloat16 [8, 64, 64, 256], P('video', 'seq')
Inputs may be any that keep to these rules, and one draw needn't show every extreme that they name: `counts`: some video has 2 earlier spans and some has none. `tile_lists`: among the tiles of one device no decoder index appears more than 2 times; some device assigns exactly 2 tiles to one decoder.
All inputs are finite; a program needn't handle non-finite values.
Results may differ from a plain program's by a relative error of at most 0.006.
Values may be sent and summed in bfloat16 or wider, within the bound.
A program may use at most 128 MiB of HBM per device.

v0:
```python
import math

import jax
import jax.numpy as jnp
from jax import lax
from jax.sharding import PartitionSpec as P

QH = 24
KVH = 4
HD = 128
LC = 16
CH = 256
TPF = 4
PAST = 2
TS = 4
CAP = 2


def noise_level(fraction):
    return 5.0 * fraction / (1.0 + 4.0 * fraction)


def causal_conv(field, weight, first_frame):
    frame_count = field.shape[1]
    height = field.shape[2]
    breadth = field.shape[3]
    channels = field.shape[4]
    padded = jnp.pad(field, ((0, 0), (2, 0), (1, 1), (1, 1), (0, 0)))
    pieces_list = []
    for delta_t in range(3):
        for delta_y in range(3):
            for delta_x in range(3):
                pieces_list.append(
                    padded[
                        :,
                        first_frame + delta_t : frame_count + delta_t,
                        delta_y : delta_y + height,
                        delta_x : delta_x + breadth,
                        :,
                    ]
                )
    stacked = jnp.concatenate(pieces_list, axis=-1)
    product = jnp.dot(
        stacked.reshape(-1, 27 * channels), weight, preferred_element_type=jnp.float32
    )
    return product.reshape(
        field.shape[0], frame_count - first_frame, height, breadth, weight.shape[1]
    )


def decode_tiles(latent_tiles, conv_in_weight, conv_weight, norm_gain):
    hidden = causal_conv(latent_tiles, conv_in_weight, 0).astype(jnp.bfloat16)
    hidden = lax.optimization_barrier(hidden)
    hidden_wide = hidden.astype(jnp.float32)
    mean_square = jnp.mean(hidden_wide * hidden_wide, axis=-1, keepdims=True)
    activated = jax.nn.silu(hidden_wide * lax.rsqrt(mean_square + 1e-06) * norm_gain).astype(
        jnp.bfloat16
    )
    mixed = causal_conv(activated, conv_weight, PAST)
    result = (hidden_wide[:, PAST:] + mixed).astype(jnp.bfloat16)
    return result.reshape(result.shape[0], TPF * TS * TS, result.shape[-1])


def attend_rows(running, grouped_queries, key_rows, valid):
    maximum, total, accumulated = running
    row_count = key_rows.shape[0]
    key_heads = key_rows[:, : KVH * HD].reshape(row_count, KVH, HD)
    value_heads = key_rows[:, KVH * HD :].reshape(row_count, KVH, HD)
    scores = jnp.einsum(
        "qgjd,kgd->gjqk", grouped_queries, key_heads, preferred_element_type=jnp.float32
    ) * (1.0 / math.sqrt(HD))
    if valid is not None:
        scores = jnp.where(valid[None, None, None, :], scores, -1e30)
    new_maximum = jnp.maximum(maximum, jnp.max(scores, axis=-1))
    correction = jnp.exp(maximum - new_maximum)
    weights = jnp.exp(scores - new_maximum[..., None])
    if valid is not None:
        weights = jnp.where(valid[None, None, None, :], weights, 0.0)
    total = total * correction + jnp.sum(weights, axis=-1)
    contribution = jnp.einsum(
        "gjqk,kgd->gjqd",
        weights.astype(jnp.bfloat16),
        value_heads,
        preferred_element_type=jnp.float32,
    )
    accumulated = accumulated * correction[..., None] + contribution
    return (new_maximum, total, accumulated)


def attend_piece(running, grouped_queries, key_rows, valid):
    row_count = key_rows.shape[0]
    for begin in range(0, row_count, 512):
        finish = min(row_count, begin + 512)
        block_valid = None if valid is None else valid[begin:finish]
        running = attend_rows(running, grouped_queries, key_rows[begin:finish], block_valid)
    return running


def on_device(
    queries,
    kv_current,
    kv_history,
    noisy_latent,
    head_weight,
    timesteps,
    counts,
    past_latent,
    tile_lists,
    conv_in_weight,
    conv_weight,
    norm_gain,
):
    token_count = queries.shape[1]
    group_size = QH // KVH
    decoders = lax.axis_size("video")
    history_count = counts[0]
    destination = tile_lists[0, :, 0]
    onehot = (destination[:, None] == jnp.arange(decoders, dtype=jnp.int32)[None, :]).astype(
        jnp.int32
    )
    earlier = jnp.cumsum(onehot, axis=0, dtype=jnp.int32) - onehot
    slot_rank = jnp.sum(earlier * onehot, axis=1, dtype=jnp.int32)
    to_decoder = destination[None, None, :] == jnp.arange(decoders, dtype=jnp.int32)[:, None, None]
    to_slot = slot_rank[None, None, :] == jnp.arange(CAP, dtype=jnp.int32)[None, :, None]
    selector = (to_decoder & to_slot).astype(jnp.bfloat16)
    past_tiles = past_latent[0]
    grouped_queries = queries[0].reshape(token_count, KVH, group_size, HD)
    running = (
        jnp.full((KVH, group_size, token_count), -1e30, jnp.float32),
        jnp.zeros((KVH, group_size, token_count), jnp.float32),
        jnp.zeros((KVH, group_size, token_count, HD), jnp.float32),
    )
    running = attend_piece(
        running, grouped_queries, lax.all_gather(kv_current[0], "seq", axis=0, tiled=True), None
    )
    fragment = lax.all_gather(kv_history[0], "seq", axis=1, tiled=True)
    slot_count = fragment.shape[0]
    row_count = fragment.shape[1]
    flattened = fragment.reshape(slot_count * row_count, fragment.shape[2])
    valid = jnp.arange(slot_count * row_count, dtype=jnp.int32) // row_count < history_count
    running = attend_piece(running, grouped_queries, flattened, valid)
    attended = running[2] / running[1][..., None]
    attended = (
        jnp.transpose(attended, (2, 0, 1, 3)).reshape(token_count, QH * HD).astype(jnp.bfloat16)
    )
    velocity = jnp.dot(attended, head_weight, preferred_element_type=jnp.float32)
    fraction = timesteps[0].astype(jnp.float32) / 1000.0
    step_size = noise_level(fraction - 0.25) - noise_level(fraction)
    next_latent = (noisy_latent[0] + step_size * velocity).astype(jnp.bfloat16)
    tile_count = past_tiles.shape[0]
    half_side = TS // 2
    shaped = next_latent.reshape(tile_count, TPF, half_side, half_side, 2, 2, LC)
    new_tiles = jnp.transpose(shaped, (0, 1, 2, 4, 3, 5, 6)).reshape(tile_count, TPF * TS * TS * LC)
    payload = jnp.concatenate([past_tiles, new_tiles], axis=-1)
    send_buffer = jnp.einsum(
        "dct,tp->dcp", selector, payload, preferred_element_type=jnp.float32
    ).astype(jnp.bfloat16)
    arrived = lax.all_to_all(send_buffer, "video", split_axis=0, concat_axis=0, tiled=True)
    sources = arrived.shape[0]
    items = arrived.shape[1]
    result = decode_tiles(
        arrived.reshape(sources * items, PAST + TPF, TS, TS, LC),
        conv_in_weight,
        conv_weight,
        norm_gain,
    )
    decoded = result.reshape(sources, items, TPF * TS * TS, result.shape[-1])
    return (next_latent[None], decoded.reshape(1, decoders * CAP, TPF * TS * TS, CH))


def solution(mesh):
    return jax.shard_map(
        on_device,
        mesh=mesh,
        in_specs=(
            P("video", "seq", None),
            P("video", "seq", None),
            P("video", None, "seq", None),
            P("video", "seq", None),
            P(),
            P("video"),
            P("video"),
            P("video", "seq", None),
            P("video", "seq", None),
            P(),
            P(),
            P(),
        ),
        out_specs=(P("video", "seq", None), P("video", "seq", None, None)),
        check_vma=False,
    )
```

profile of v0, /device:TPU:0, one launch (start us, length us, event | category | flops | bytes accessed | tf_op | source)
XLA Modules:
  0.0 155.2 jit_solution(8332041722420638009)
XLA Ops:
  7.2 1.9 %copy.61 = bf16[1,128,1024]{1,2,0:T(8,128)(2,1)} copy(bf16[1,128,1024]{2,1,0:T(8,128)(2,1)} %param.13) | data formatting | bytes 524288 | tf_op args[1]
  9.2 2.0 %copy.66 = bf16[1,2,128,1024]{2,3,1,0:T(8,128)(2,1)} copy(bf16[1,2,128,1024]{3,2,1,0:T(8,128)(2,1)} %param.14) | data formatting | bytes 1048576 | tf_op args[2]
  11.9 2.3 %copy.62 = bf16[1,128,3072]{1,2,0:T(8,128)(2,1)} copy(bf16[1,128,3072]{2,1,0:T(8,128)(2,1)} %param.12) | data formatting | bytes 1572864 | tf_op args[0]
  18.2 24.3 %all-gather.5.cloned.1.call-done = bf16[1,512,1024]{1,2,0:T(8,128)(2,1)} async-done(((bf16[1,128,1024]{1,2,0:T(8,128)(2,1)}), bf16[1,512,1024]{1,2,0:T(8,128)(2,1)}) %all-gather.5.cloned.1.call-update) | async-done | bytes 1048592 | tf_op jit(solution)/shard_map/all_gather | solution.py:134
  42.5 2.1 %fusion.93 = (bf16[512,512]{0,1:T(8,128)(2,1)}, bf16[512,512]{0,1:T(8,128)(2,1)S(1)}) fusion(bf16[512,1024]{0,1:T(8,128)(2,1)} %bitcast.185), kind=kLoop, calls=%fused_computation.171 | loop fusion | bytes 2097152 | tf_op jit(solution)/shard_map/slice | solution.py:68
  44.6 4.8 %bitcast_reduce_fusion.2 = (f32[4,6,128]{2,1,0:T(8,128)S(1)}, f32[4,512,128,6]{2,1,3,0:T(8,128)}) fusion(bf16[512,4,128,1]{0,2,3,1:T(8,128)(2,1)S(1)} %bitcast.182, bf16[128,4,6,128]{0,3,2,1:T(8,128)(2,1)} %bitcast.178), kind=kOutput, calls=%fused_computation.59 | convolution fusion | flops 405795840 | bytes 7614464 | tf_op jit(solution)/shard_map/qgjd,kgd->gjqk/dot_general | solution.py:69
  49.4 39.8 %all-gather.7.cloned.1.call-done = bf16[1,2,512,1024]{2,3,1,0:T(8,128)(2,1)} async-done(((bf16[1,2,128,1024]{2,3,1,0:T(8,128)(2,1)}), bf16[1,2,512,1024]{2,3,1,0:T(8,128)(2,1)}) %all-gather.7.cloned.1.call-update) | async-done | bytes 2097168 | tf_op jit(solution)/shard_map/all_gather | solution.py:136
  89.2 1.7 %slice_bitcast_fusion.1 = (bf16[512,1024]{0,1:T(8,128)(2,1)S(1)}, bf16[512,1024]{0,1:T(8,128)(2,1)S(1)}) fusion(bf16[1,2,512,1024]{2,3,1,0:T(8,128)(2,1)} %all-gather.7.cloned.1.call-done), kind=kLoop, calls=%fused_computation.97 | loop fusion | bytes 4194304 | tf_op jit(solution)/shard_map/slice | solution.py:95
  91.2 1.5 bitcast_reduce_fusion
  92.6 1.5 bitcast_reduce_fusion.1
  94.2 2.0 %fusion.9 = f32[4,6,128]{2,1,0:T(8,128)S(1)} fusion(f32[4,512,128,6]{2,1,3,0:T(8,128)S(1)} %get-tuple-element.56, f32[4,6,128]{2,1,0:T(8,128)S(1)} %get-tuple-element.12, pred[512]{0:T(512)(128)(4,1)S(1)} %copy-done.8), kind=kLoop, calls=%fused_computation.67 | loop fusion | flops 7861248 | bytes 6316544 | tf_op jit(solution)/shard_map/reduce_sum | solution.py:79
  96.2 1.7 %fusion.17 = f32[4,6,128,128]{2,3,1,0:T(8,128)S(1)} fusion(bf16[512,4,128,1]{0,2,3,1:T(8,128)(2,1)S(1)} %bitcast.190, f32[4,512,128,6]{2,1,3,0:T(8,128)S(1)} %get-tuple-element.56, f32[4,6,128]{2,1,0:T(8,128)S(1)} %get-tuple-element.12, pred[512]{0:T(512)(128)(4,1)S(1)} %copy-done.8), kind=kOutput, calls=%fused_computation.74 | convolution fusion | flops 410517504 | bytes 8401408 | tf_op jit(solution)/shard_map/gjqk,kgd->gjqd/dot_general | solution.py:80
  101.5 1.8 %fusion.7 = f32[4,6,128]{2,1,0:T(8,128)S(1)} fusion(f32[4,512,128,6]{2,1,3,0:T(8,128)S(1)} %get-tuple-element.58, f32[4,6,128]{2,1,0:T(8,128)S(1)} %get-tuple-element.13, pred[512]{0:T(512)(128)(4,1)S(1)} %copy-done.7), kind=kLoop, calls=%fused_computation.65 | loop fusion | flops 7861248 | bytes 6316544 | tf_op jit(solution)/shard_map/reduce_sum | solution.py:79
  103.4 2.0 %fusion.26 = bf16[128,4,6,128]{0,3,2,1:T(8,128)(2,1)S(1)} fusion(f32[4,6,128,128]{2,3,1,0:T(8,128)S(1)} %fusion.17, f32[4,6,128,128]{2,3,1,0:T(8,128)S(1)} %fusion.13, bf16[512,4,128,1]{0,2,3,1:T(8,128)(2,1)S(1)} %bitcast.189, f32[4,512,128,6]{2,1,3,0:T(8,128)S(1)} %get-tuple-element.58, f32[4,6,128]{2,1,0:T(8,128)S(1)} %get-tuple-element.13, ...), kind=kOutput, calls=%fused_computation.83 | convolution fusion | flops 413270016 | bytes 10809856 | tf_op jit(solution)/shard_map/gjqk,kgd->gjqd/dot_general | solution.py:80
  106.5 1.5 reshape.259
  108.0 1.6 %copy.74 = bf16[8,4,2,2,2,2,16]{6,5,4,3,2,1,0:T(2,128)(2,1)} copy(bf16[8,4,2,2,2,2,16]{6,5,3,4,2,1,0:T(2,128)(2,1)} %bitcast.187) | data formatting | bytes 32768 | tf_op jit(solution)/shard_map/transpose | solution.py:153
  109.6 1.7 %reshape.260 = bf16[8,1024]{1,0:T(8,128)(2,1)} reshape(bf16[8,4,2,2,2,2,16]{6,5,4,3,2,1,0:T(2,128)(2,1)} %copy.74) | data formatting | bytes 32768 | tf_op jit(solution)/shard_map/reshape | solution.py:153
  112.2 8.5 %all_to_all.5 = bf16[8,2,1536]{2,1,0:T(2,128)(2,1)} all-to-all(bf16[8,2,1536]{2,1,0:T(2,128)(2,1)S(1)} %copy.75), channel_id=1, replica_groups=mesh['seq'=4,'video'=8] {'video'}, dimensions={0} | all-to-all | bytes 98304 | tf_op jit(solution)/shard_map/all_to_all | solution.py:158
  120.8 1.9 %reshape.261 = bf16[16,6,4,4,16]{4,3,2,1,0:T(4,128)(2,1)} reshape(bf16[8,2,1536]{2,1,0:T(2,128)(2,1)} %all_to_all.5) | data formatting | bytes 98304 | tf_op jit(solution)/shard_map/reshape | solution.py:162
  123.8 3.3 %pad_slice_fusion.24 = (bf16[16,6,4,4,16]{4,0,3,2,1:T(8,128)(2,1)}, bf16[16,6,4,4,16]{4,0,3,2,1:T(8,128)(2,1)}, bf16[16,6,4,4,16]{4,0,3,2,1:T(8,128)(2,1)}, bf16...) fusion(bf16[16,6,4,4,16]{4,0,3,2,1:T(8,128)(2,1)S(1)} %copy.76), kind=kLoop, calls=%fused_computation.24 | loop fusion | bytes 983040 | tf_op jit(solution)/shard_map/slice | solution.py:34
  127.1 1.8 %pad_slice_fusion.25 = (bf16[16,6,4,4,16]{4,0,3,2,1:T(8,128)(2,1)}, bf16[16,6,4,4,16]{4,0,3,2,1:T(8,128)(2,1)}, bf16[16,6,4,4,16]{4,0,3,2,1:T(8,128)(2,1)}, bf16...) fusion(bf16[16,6,4,4,16]{4,0,3,2,1:T(8,128)(2,1)S(1)} %copy.76), kind=kLoop, calls=%fused_computation.25 | loop fusion | bytes 393216 | tf_op jit(solution)/shard_map/slice | solution.py:34
  129.0 10.2 %concatenate.12 = bf16[16,6,4,4,432]{4,0,3,2,1:T(8,128)(2,1)} concatenate(bf16[16,6,4,4,16]{4,0,3,2,1:T(8,128)(2,1)} %get-tuple-element.47, bf16[16,6,4,4,16]{4,0,3,2,1:T(8,128)(2,1)} %get-tuple-element.23, bf16[16,6,4,4,16]{4,0,3,2,1:T(8,128)(2,1)} %get-tuple-element.24, bf16[16,6,4,4,16]{4,0,3,2,1:T(8,128)(2,1)} %get-tuple-element.25, ...), dimensions={4} | concatenate | bytes 2654208 | tf_op jit(solution)/shard_map/concatenate | solution.py:42
  139.1 2.0 %convolution_convert_fusion.1 = bf16[16,6,4,4,256]{4,0,3,2,1:T(8,128)(2,1)S(1)} fusion(bf16[16,6,4,4,432]{4,0,3,2,1:T(8,128)(2,1)} %concatenate.12, bf16[432,256]{1,0:T(8,128)(2,1)} %param.21), kind=kOutput, calls=%fused_computation.90 | convolution fusion | flops 340131840 | bytes 2334720 | tf_op jit(solution)/shard_map/dot_general | solution.py:43
  143.6 3.8 %fusion.34 = bf16[16,4,4,4,256]{4,0,3,2,1:T(8,128)(2,1)S(1)} fusion(bf16[16,4,4,4,6912]{4,0,3,2,1:T(8,128)(2,1)S(1)} %fusion.62, bf16[6912,256]{1,0:T(8,128)(2,1)S(1)} %copy-done, f32[16,6,4,4,256]{4,0,3,2,1:T(8,128)S(1)} %convert_element_type.55), kind=kOutput, calls=%fused_computation.92 | convolution fusion | flops 3624402944 | bytes 19267584 | tf_op jit(solution)/shard_map/dot_general | solution.py:43
  (77 shorter events, 13.3 us)
Async XLA Ops:
  7.2 136.4 %copy-start = (bf16[6912,256]{1,0:T(8,128)(2,1)S(1)}, bf16[6912,256]{1,0:T(8,128)(2,1)}, u32[]{:S(2)}) copy-start(bf16[6912,256]{1,0:T(8,128)(2,1)} %param.22) | copy-start | bytes 10616836
  7.2 35.3 %all-gather.5.cloned.1.call-start = ((), (), s32[]{:S(2)}) async-start(), calls=%async_computation.1 | async-start | bytes 1310720 | tf_op jit(solution)/shard_map/all_gather | solution.py:134
  9.2 80.0 %all-gather.7.cloned.1.call-start = ((), (), s32[]{:S(2)}) async-start(), calls=%async_computation.2 | async-start | bytes 2621440 | tf_op jit(solution)/shard_map/all_gather | solution.py:136
  89.2 1.9 %copy-start.1 = (bf16[1,128,3072]{1,2,0:T(8,128)(2,1)S(1)}, bf16[1,128,3072]{1,2,0:T(8,128)(2,1)}, u32[]{:S(2)}) copy-start(bf16[1,128,3072]{1,2,0:T(8,128)(2,1)} %copy.62) | copy-start | bytes 2359300
  89.2 1.9 %copy-start.8 = (pred[512]{0:T(512)(128)(4,1)S(1)}, pred[512]{0:T(512)(128)(4,1)}, u32[]{:S(2)}) copy-start(pred[512]{0:T(512)(128)(4,1)} %get-tuple-element.52) | copy-start | bytes 1540
  91.0 1.7 %copy-start.7 = (pred[512]{0:T(512)(128)(4,1)S(1)}, pred[512]{0:T(512)(128)(4,1)}, u32[]{:S(2)}) copy-start(pred[512]{0:T(512)(128)(4,1)} %get-tuple-element.51) | copy-start | bytes 1540
  96.2 2.3 %slice-start = ((s8[6291456]{0:T(1024)(128)(4,1)}), s8[4194304]{0:T(1024)(128)(4,1)S(1)}, s32[]{:S(2)}) async-start(s8[6291456]{0:T(1024)(128)(4,1)} %bitcast.176), calls=%async_computation.3 | async-start | bytes 8388608
  96.2 3.0 %slice-start.1 = ((s8[6291456]{0:T(1024)(128)(4,1)}), s8[2097152]{0:T(1024)(128)(4,1)S(1)}, s32[]{:S(2)}) async-start(s8[6291456]{0:T(1024)(128)(4,1)} %bitcast.176), calls=%async_computation.4 | async-start | bytes 4194304
  96.2 4.1 %copy-start.3 = (bf16[512,512]{0,1:T(8,128)(2,1)S(1)}, bf16[512,512]{0,1:T(8,128)(2,1)}, u32[]{:S(2)}) copy-start(bf16[512,512]{0,1:T(8,128)(2,1)} %get-tuple-element.18) | copy-start | bytes 1572868
  103.4 2.1 %copy-start.4 = (bf16[3072,64]{0,1:T(8,128)(2,1)S(1)}, bf16[3072,64]{0,1:T(8,128)(2,1)}, u32[]{:S(2)}) copy-start(bf16[3072,64]{0,1:T(8,128)(2,1)} %param.16) | copy-start | bytes 1179652
  103.4 2.1 %copy-start.6 = (f32[1,128,64]{1,2,0:T(8,128)S(1)}, f32[1,128,64]{1,2,0:T(8,128)}, u32[]{:S(2)}) copy-start(f32[1,128,64]{1,2,0:T(8,128)} %param.15) | copy-start | bytes 98308
  105.7 23.2 %copy-start.5 = (bf16[128,64]{0,1:T(8,128)(2,1)}, bf16[128,64]{0,1:T(8,128)(2,1)S(1)}, u32[]{:S(2)}) copy-start(bf16[128,64]{0,1:T(8,128)(2,1)S(1)} %fusion.38) | copy-start | bytes 49156
  123.8 3.4 %copy-start.2 = (bf16[16,6,4,4,16]{4,0,3,2,1:T(8,128)(2,1)}, bf16[16,6,4,4,16]{4,0,3,2,1:T(8,128)(2,1)S(1)}, u32[]{:S(2)}) copy-start(bf16[16,6,4,4,16]{4,0,3,2,1:T(8,128)(2,1)S(1)} %copy.76) | copy-start | bytes 147460
  129.0 12.7 %copy-start.9 = (f32[256]{0:T(256)S(1)}, f32[256]{0:T(256)}, u32[]{:S(2)}) copy-start(f32[256]{0:T(256)} %param.23) | copy-start | bytes 3076
Sparse Core Ops, SparseCore 0:
  9.6 32.8 all-gather.4
  44.6 44.5 all-gather.6
where the time goes:
time: 157 us; the launch traced here: 155 us
  waiting for transfers between devices  64.1 us (41%)
  local copies, waits for them, and re-layouts  38.1 us (24%)
  matrix products  19.7 us (13%)
  between operations  15.9 us (10%)
  other arithmetic  8.64 us (6%)
  blocking collectives  8.53 us (5%)
    all_gather x1, waiting for transfers between devices, on_device(): fragment = lax.all_gather(kv_history[0], 'seq', axis=1, tiled=True)  39.8 us
    all_gather x1, waiting for transfers between devices, on_device(): lax.all_gather(kv_current[0], 'seq', axis=0, tiled=True)  24.3 us
    concatenate x2, local copies, waits for them, and re-layouts, causal_conv(): stacked = jnp.concatenate(pieces_list, axis=-1)  10.2 us
    unnamed x54, local copies, waits for them, and re-layouts  9.64 us
    all_to_all x1, blocking collectives, on_device(): lax.all_to_all(send_buffer, 'video', split_axis=0, concat_axis=0, tiled=T...  8.53 us
    dot_general x3, matrix products, attend_rows(): jnp.einsum('qgjd,kgd->gjqk', grouped_queries, key_heads, preferred_elemen...  7.77 us
    dot_general x2, matrix products, causal_conv(): jnp.dot(stacked.reshape(-1, 27 * channels), weight, preferred_element_typ...  5.79 us
    slice x2, local copies, waits for them, and re-layouts, causal_conv(): padded[:, first_frame + delta_t:frame_count + delta_t, delta_y:delta_y +...  5.15 us
  transfers between devices with their start and end apart: 2, of which 2 were waited for; matrix products, arithmetic and copies ran while one was open for 9% of the time, Pallas kernels for 0%

commit v1 on v0

v1 whole, which is shorter than its diff:
```python
import functools
import math

import jax
import jax.numpy as jnp
from jax import lax
from jax.experimental import pallas as pl
from jax.experimental.pallas import tpu as pltpu
from jax.sharding import PartitionSpec as P

QH = 24
KVH = 4
HD = 128
LC = 16
CH = 256
TPF = 4
PAST = 2
TS = 4
CAP = 2
FRAMES = PAST + TPF
CELLS = TS * TS
WIDE = CELLS * LC
PACK = 16
MESH = pl.DeviceIdType.MESH
F32 = jnp.float32
BF16 = jnp.bfloat16


def noise_level(fraction):
    return 5.0 * fraction / (1.0 + 4.0 * fraction)


def iota(shape, axis):
    return lax.broadcasted_iota(jnp.int32, shape, axis)


def one_hot(condition):
    return jnp.where(condition, 1.0, 0.0).astype(BF16)


def dot(a, b):
    return jnp.dot(a, b, preferred_element_type=F32)


def step_kernel(
    n_seq,
    n_video,
    q_ref,
    kvc_ref,
    kvh_ref,
    noisy_ref,
    hw_ref,
    ts_ref,
    counts_ref,
    past_ref,
    lists_ref,
    win_ref,
    w2_ref,
    gain_ref,
    nl_ref,
    dec_ref,
    q_all,
    k_all,
    v_all,
    k_use,
    v_use,
    w_raw,
    w_low,
    w_high,
    vel_out,
    vel_in,
    win,
    w2,
    toeplitz,
    tiles_out,
    tiles_in,
    field,
    acc,
    kv_send,
    kv_recv,
    q_send,
    q_recv,
    vel_send,
    vel_recv,
    tile_send,
    tile_recv,
    own_sem,
):
    me = lax.axis_index("seq")
    mv = lax.axis_index("video")
    heads = QH // n_seq
    group = QH // KVH
    slots = kvh_ref.shape[0] + 1
    tokens = q_ref.shape[0]
    half = tokens // 2
    tile_count = tokens // (TPF * 4)
    rows = n_video * CAP

    def seq_peer(k):
        if n_seq == 4:
            return (me + 1 - 2 * (me % 2), (me + 2) % 4, 3 - me)[k - 1]
        return (me + k) % n_seq

    def video_peer(k):
        return (mv + k) % n_video

    barrier = pltpu.get_barrier_semaphore()
    for k in range(1, n_seq):
        pl.semaphore_signal(barrier, inc=1, device_id=(seq_peer(k), mv), device_id_type=MESH)
    for k in range(1, n_video):
        pl.semaphore_signal(barrier, inc=1, device_id=(me, video_peer(k)), device_id_type=MESH)
    pl.semaphore_wait(barrier, n_seq + n_video - 2)

    def kv_parts(target, owner):
        column = pl.multiple_of((target * heads // group) * HD, HD)
        key_columns = pl.ds(column, HD)
        value_columns = pl.ds(pl.multiple_of(column + KVH * HD, HD), HD)
        return (
            (kvc_ref.at[:, key_columns], k_all.at[owner, 0]),
            (kvh_ref.at[:, :, key_columns], k_all.at[owner, pl.ds(1, slots - 1)]),
            (kvc_ref.at[:, value_columns], v_all.at[owner, 0]),
            (kvh_ref.at[:, :, value_columns], v_all.at[owner, pl.ds(1, slots - 1)]),
        )

    def kv_copy(target, owner, part):
        source, place = kv_parts(target, owner)[part]
        return pltpu.make_async_remote_copy(
            source,
            place,
            kv_send.at[target, part],
            kv_recv.at[owner, part],
            device_id=(target, mv),
            device_id_type=MESH,
        )

    def q_part(target, owner, head):
        column = pl.multiple_of((target * heads + head) * HD, HD)
        return q_ref.at[:, pl.ds(column, HD)], q_all.at[owner, head]

    def q_copy(target, owner, head):
        source, place = q_part(target, owner, head)
        return pltpu.make_async_remote_copy(
            source,
            place,
            q_send.at[target, head],
            q_recv.at[owner, head],
            device_id=(target, mv),
            device_id_type=MESH,
        )

    def vel_copy(target, owner):
        return pltpu.make_async_remote_copy(
            vel_out.at[target],
            vel_in.at[owner],
            vel_send.at[target],
            vel_recv.at[owner],
            device_id=(target, mv),
            device_id_type=MESH,
        )

    def tile_copy(target, owner):
        return pltpu.make_async_remote_copy(
            tiles_out.at[target],
            tiles_in.at[owner],
            tile_send.at[target],
            tile_recv.at[owner],
            device_id=(me, target),
            device_id_type=MESH,
        )

    send_order = range(n_seq - 1, 0, -1)
    for k in send_order:
        for part in range(4):
            kv_copy(seq_peer(k), me, part).start()

    for k in send_order:
        target = seq_peer(k)

        def send_head(head, carry, target=target):
            q_copy(target, me, head).start()
            return carry

        lax.fori_loop(0, heads, send_head, 0)

    own = []
    for part, (source, place) in enumerate(kv_parts(me, me)):
        own.append(pltpu.make_async_copy(source, place, own_sem.at[part]))
    for head in range(heads):
        source, place = q_part(me, me, head)
        own.append(pltpu.make_async_copy(source, place, own_sem.at[4 + head]))
    w_rows = pl.ds(pl.multiple_of(me * heads * HD, HD), heads * HD)
    own.append(pltpu.make_async_copy(hw_ref.at[w_rows], w_raw, own_sem.at[4 + heads]))
    own.append(pltpu.make_async_copy(win_ref, win, own_sem.at[5 + heads]))
    own.append(pltpu.make_async_copy(w2_ref, w2, own_sem.at[6 + heads]))
    for copy in own:
        copy.start()

    width = w_raw.shape[1]
    own[4 + heads].wait()
    shape = (width, 2 * width)
    w_low[...] = dot(w_raw[...], one_hot(iota(shape, 1) == iota(shape, 0))).astype(BF16)
    w_high[...] = dot(w_raw[...], one_hot(iota(shape, 1) == iota(shape, 0) + width)).astype(BF16)

    def clear(cell, carry):
        toeplitz[cell] = jnp.zeros(toeplitz.shape[1:], BF16)
        return carry

    lax.fori_loop(0, CELLS, clear, 0)
    own[5 + heads].wait()
    for y in range(TS):
        for x in range(TS):
            first = max(0, x - 1)
            count = min(TS, x + 2) - first
            for yy in range(max(0, y - 1), min(TS, y + 2)):
                to = (yy * TS + first) * LC
                start = ((yy - y + 1) * 3 + first - x + 1) * LC
                toeplitz[y * TS + x, :, to : to + count * LC, :] = win[:, start : start + count * LC, :]

    token_code = jnp.zeros((1, tokens), jnp.int32)
    past_code = jnp.zeros((1, PAST * tile_count), jnp.int32)
    token_tile = iota((1, tokens), 1) // (TPF * 4)
    past_tile = iota((1, PAST * tile_count), 1) % tile_count
    for t in range(tile_count):
        code = lists_ref[t] * CAP
        for t2 in range(t):
            code = code + jnp.where(lists_ref[t2] == lists_ref[t], 1, 0)
        token_code = jnp.where(token_tile == t, code, token_code)
        past_code = jnp.where(past_tile == t, code, past_code)
    out_rows = n_video * PACK

    def row_match(columns, code, frame):
        row = iota((out_rows, columns), 0)
        place = row % PACK
        row_code = (row // PACK) * CAP + place % CAP
        return one_hot((row_code == code) & (place // CAP == frame))

    token_match = row_match(tokens, token_code, iota((1, tokens), 1) // 4 % TPF + PAST)
    past_match = row_match(
        PAST * tile_count, past_code, iota((1, PAST * tile_count), 1) // tile_count
    )
    past_wide = past_ref[...].astype(F32)
    past_rows = jnp.concatenate(
        [past_wide[:, f * WIDE : (f + 1) * WIDE] for f in range(PAST)], axis=0
    ).astype(BF16)
    past_sent = dot(past_match, past_rows)

    shape = (2 * width, WIDE)
    lane = iota(shape, 1)
    cell = lane // LC
    wanted = (cell // TS % 2 * 2 + cell % 2) * LC + lane % LC
    spread_low = one_hot(iota(shape, 0) == wanted)
    spread_high = one_hot(iota(shape, 0) == wanted + width)
    shape = (tokens, WIDE)
    cell = iota(shape, 1) // LC
    in_place = iota(shape, 0) % 4 == cell // TS // 2 * 2 + cell % TS // 2

    noisy = noisy_ref[...]
    noisy = jnp.concatenate([noisy[:half], noisy[half:]], axis=1)
    fraction = jnp.full((half, 2 * width), ts_ref[0], jnp.int32).astype(F32) / 1000.0
    step_size = noise_level(fraction - 0.25) - noise_level(fraction)

    held = jnp.full((tokens, HD), counts_ref[0], jnp.int32)

    def take_rows(source):
        key_rows = k_all[source, 0]
        k_use[source, 0] = key_rows
        v_use[source, 0, :, :HD] = v_all[source, 0]
        v_use[source, 0, :, HD:] = jnp.ones((tokens, HD), BF16)
        for slot in range(1, slots):
            valid = held >= slot
            k_use[source, slot] = jnp.where(
                valid, k_all[source, slot].astype(F32), key_rows.astype(F32)
            ).astype(BF16)
            v_use[source, slot, :, :HD] = jnp.where(
                valid, v_all[source, slot].astype(F32), 0.0
            ).astype(BF16)
            v_use[source, slot, :, HD:] = jnp.where(valid, 1.0, 0.0).astype(BF16)

    for part in range(4):
        own[part].wait()
    take_rows(me)
    for k in range(1, n_seq):
        source = seq_peer(k)
        for part in range(4):
            kv_copy(me, source, part).wait_recv()
        take_rows(source)

    scale = math.log2(math.e) / math.sqrt(HD)
    key_count = n_seq * slots * tokens

    def attend(source, head):
        keys = k_use[...].reshape(key_count, HD)
        scores = lax.dot_general(
            q_all[source, head], keys, (((1,), (1,)), ((), ())), preferred_element_type=F32
        )
        top = jnp.max(scores, axis=-1, keepdims=True)
        weights = jnp.exp2((scores - top) * scale).astype(BF16)
        mixed = dot(weights, v_use[...].reshape(key_count, 2 * HD))
        attended = (mixed[:, :HD] / mixed[:, HD:]).astype(BF16)
        columns = pl.ds(pl.multiple_of(head * HD, HD), HD)
        return dot(attended[:half], w_low[columns]) + dot(attended[half:], w_high[columns])

    for head in range(heads):
        own[4 + head].wait()
    zero = jnp.zeros((half, 2 * width), F32)
    vel_in[me] = lax.fori_loop(0, heads, lambda h, total: total + attend(me, h), zero)
    for k in range(1, n_seq):
        source = seq_peer(k)

        def one_head(head, total, source=source):
            q_copy(me, source, head).wait_recv()
            return total + attend(source, head)

        vel_out[source] = lax.fori_loop(0, heads, one_head, zero)
        vel_copy(source, me).start()

    for k in range(1, n_seq):
        vel_copy(me, seq_peer(k)).wait_recv()
    velocity = vel_in[0]
    for k in range(1, n_seq):
        velocity = velocity + vel_in[k]
    latent = (noisy + step_size * velocity).astype(BF16)

    spread = jnp.concatenate([dot(latent, spread_low), dot(latent, spread_high)], axis=0)
    spread = jnp.where(in_place, spread, 0.0).astype(BF16)
    tiles_out[...] = (
        (dot(token_match, spread) + past_sent).astype(BF16).reshape(n_video, PACK, WIDE)
    )
    for k in range(1, n_video):
        tile_copy(video_peer(k), mv).start()
    tiles_in[mv] = tiles_out[mv]
    nl_ref[:half] = latent[:, :width]
    nl_ref[half:] = latent[:, width:]

    shape = ((PAST + FRAMES) * rows, n_video * PACK)
    row = iota(shape, 0)
    item = row % rows
    frame = row // rows - PAST
    gather = one_hot(
        (iota(shape, 1) == item // CAP * PACK + frame * CAP + item % CAP) & (frame >= 0)
    )
    own[6 + heads].wait()
    for k in range(1, n_video):
        tile_copy(mv, video_peer(k)).wait_recv()
    frames = dot(gather, tiles_in[...].reshape(n_video * PACK, WIDE)).astype(BF16)
    taps = jnp.concatenate(
        [frames[dt * rows : (dt + FRAMES) * rows] for dt in range(3)], axis=1
    )

    def first_conv(cell, carry):
        hidden = dot(taps, toeplitz[cell].reshape(3 * WIDE, CH)).astype(BF16)
        wide = hidden.astype(F32)
        mean_square = jnp.mean(wide * wide, axis=-1, keepdims=True)
        unit = wide * lax.rsqrt(mean_square + 1e-06) * gain_ref[...]
        active = unit / (1.0 + jnp.exp(-unit))
        y, x = cell // TS, cell % TS
        field[y, x] = active.astype(BF16).reshape(FRAMES, rows, CH)
        acc[y, x] = wide[PAST * rows :].reshape(TPF, rows, CH)
        return carry

    lax.fori_loop(0, CELLS, first_conv, 0)

    for dy in range(3):
        for dx in range(3):
            y0, x0 = max(0, 1 - dy), max(0, 1 - dx)
            ny, nx = TS - abs(dy - 1), TS - abs(dx - 1)
            ys, xs = y0 + dy - 1, x0 + dx - 1
            lhs = jnp.concatenate(
                [
                    field[ys : ys + ny, xs : xs + nx, dt : dt + TPF].reshape(
                        ny * nx * TPF * rows, CH
                    )
                    for dt in range(3)
                ],
                axis=1,
            )
            product = dot(lhs, w2[:, dy * 3 + dx].reshape(3 * CH, CH))
            acc[y0 : y0 + ny, x0 : x0 + nx] += product.reshape(ny, nx, TPF, rows, CH)
    dec_ref[...] = acc[...].reshape(CELLS, TPF, rows, CH).astype(BF16)

    for k in range(1, n_seq):
        target = seq_peer(k)
        for part in range(4):
            kv_copy(target, me, part).wait_send()

        def sent_head(head, carry, target=target):
            q_copy(target, me, head).wait_send()
            return carry

        lax.fori_loop(0, heads, sent_head, 0)
        vel_copy(target, me).wait_send()
    for k in range(1, n_video):
        tile_copy(video_peer(k), mv).wait_send()


def on_device(
    n_seq,
    n_video,
    queries,
    kv_current,
    kv_history,
    noisy_latent,
    head_weight,
    timesteps,
    counts,
    past_latent,
    tile_lists,
    conv_in_weight,
    conv_weight,
    norm_gain,
):
    tokens = queries.shape[1]
    heads = QH // n_seq
    slots = kv_history.shape[1] + 1
    width = head_weight.shape[1]
    rows = n_video * CAP
    anywhere = pl.BlockSpec(memory_space=pl.ANY)
    vmem = pl.BlockSpec(memory_space=pltpu.VMEM)
    smem = pl.BlockSpec(memory_space=pltpu.SMEM)
    dma = pltpu.SemaphoreType.DMA
    next_latent, decoded = pl.pallas_call(
        functools.partial(step_kernel, n_seq, n_video),
        out_shape=(
            jax.ShapeDtypeStruct((tokens, width), BF16),
            jax.ShapeDtypeStruct((CELLS, TPF, rows, CH), BF16),
        ),
        in_specs=[
            anywhere,
            anywhere,
            anywhere,
            vmem,
            anywhere,
            smem,
            smem,
            vmem,
            smem,
            anywhere,
            anywhere,
            vmem,
        ],
        out_specs=(vmem, vmem),
        scratch_shapes=[
            pltpu.VMEM((n_seq, heads, tokens, HD), BF16),
            pltpu.VMEM((n_seq, slots, tokens, HD), BF16),
            pltpu.VMEM((n_seq, slots, tokens, HD), BF16),
            pltpu.VMEM((n_seq, slots, tokens, HD), BF16),
            pltpu.VMEM((n_seq, slots, tokens, 2 * HD), BF16),
            pltpu.VMEM((heads * HD, width), BF16),
            pltpu.VMEM((heads * HD, 2 * width), BF16),
            pltpu.VMEM((heads * HD, 2 * width), BF16),
            pltpu.VMEM((n_seq, tokens // 2, 2 * width), F32),
            pltpu.VMEM((n_seq, tokens // 2, 2 * width), F32),
            pltpu.VMEM((3, 9 * LC, CH), BF16),
            pltpu.VMEM((3, 9, CH, CH), BF16),
            pltpu.VMEM((CELLS, 3, WIDE, CH), BF16),
            pltpu.VMEM((n_video, PACK, WIDE), BF16),
            pltpu.VMEM((n_video, PACK, WIDE), BF16),
            pltpu.VMEM((TS, TS, FRAMES, rows, CH), BF16),
            pltpu.VMEM((TS, TS, TPF, rows, CH), F32),
            dma((n_seq, 4)),
            dma((n_seq, 4)),
            dma((n_seq, heads)),
            dma((n_seq, heads)),
            dma((n_seq,)),
            dma((n_seq,)),
            dma((n_video,)),
            dma((n_video,)),
            dma((7 + heads,)),
        ],
        compiler_params=pltpu.CompilerParams(
            collective_id=0, has_side_effects=True, vmem_limit_bytes=56 * 1024 * 1024
        ),
    )(
        queries[0],
        kv_current[0],
        kv_history[0],
        noisy_latent[0],
        head_weight,
        timesteps,
        counts,
        past_latent[0],
        tile_lists.reshape(-1),
        conv_in_weight.reshape(3, 9 * LC, CH),
        conv_weight.reshape(3, 9, CH, CH),
        norm_gain[None],
    )
    decoded = jnp.transpose(decoded, (2, 1, 0, 3)).reshape(1, rows, TPF * CELLS, CH)
    return next_latent[None], decoded


def solution(mesh):
    return jax.shard_map(
        functools.partial(on_device, mesh.shape["seq"], mesh.shape["video"]),
        mesh=mesh,
        in_specs=(
            P("video", "seq", None),
            P("video", "seq", None),
            P("video", None, "seq", None),
            P("video", "seq", None),
            P(),
            P("video"),
            P("video"),
            P("video", "seq", None),
            P("video", "seq", None),
            P(),
            P(),
            P(),
        ),
        out_specs=(P("video", "seq", None), P("video", "seq", None, None)),
        check_vma=False,
    )
```

time: 157 us -> 81.7 us (0.52)
  Pallas kernels: 0 us -> 72.2 us
  waiting for transfers between devices: 64.1 us -> 0 us
  local copies, waits for them, and re-layouts: 38.1 us -> 7.22 us
  matrix products: 19.7 us -> 0 us
  between operations: 15.9 us -> 1.93 us
  other arithmetic: 8.64 us -> 0 us
  blocking collectives: 8.53 us -> 0 us
    pallas_call x0 -> x1, Pallas kernels: none -> 72.2 us  [on_device(): pl.pallas_call(functools.partial(step_kernel, n_seq, n_video), out_shape=...]
    all_gather x2 -> x0, waiting for transfers between devices: 64.1 us -> none  [the longest x1 39.8 us: on_device(): fragment = lax.all_gather(kv_history[0], 'seq', axis=1, tiled=True)]
    dot_general x10 -> x0, matrix products: 19.7 us -> none  [the longest x3 7.77 us: attend_rows(): jnp.einsum('qgjd,kgd->gjqk', grouped_queries, key_heads, preferred_elemen...]
    concatenate x2 -> x0, local copies, waits for them, and re-layouts: 10.2 us -> none  [causal_conv(): stacked = jnp.concatenate(pieces_list, axis=-1)]
    slice x6 -> x0, local copies, waits for them, and re-layouts: 9.66 us -> none  [the longest x2 5.15 us: causal_conv(): padded[:, first_frame + delta_t:frame_count + delta_t, delta_y:delta_y +...]
    all_to_all x1 -> x0, blocking collectives: 8.53 us -> none  [on_device(): lax.all_to_all(send_buffer, 'video', split_axis=0, concat_axis=0, tiled=T...]
    reshape x4 -> x0, local copies, waits for them, and re-layouts: 6.23 us -> none  [the longest x2 3 us: on_device(): arrived.reshape(sources * items, PAST + TPF, TS, TS, LC)]
    reduce_sum x5 -> x0, other arithmetic: 6 us -> none  [the longest x3 4.85 us: attend_rows(): total = total * correction + jnp.sum(weights, axis=-1)]
  transfers between devices with their start and end apart: 2 -> 0, of which waited for: 2 -> 0; matrix products, arithmetic and copies ran while one was open for 9% -> 0% of each run, Pallas kernels for 0% -> 0%
where the time goes in v1:
time: 81.7 us; the launch traced here: 81.3 us
  Pallas kernels  72.2 us (88%)
  local copies, waits for them, and re-layouts  7.22 us (9%)
  between operations  1.93 us (2%)
    pallas_call x1, Pallas kernels, on_device(): pl.pallas_call(functools.partial(step_kernel, n_seq, n_video), out_shape=...  72.2 us
    unnamed x3, local copies, waits for them, and re-layouts  5.09 us
    transpose x1, local copies, waits for them, and re-layouts, on_device(): jnp.transpose(decoded, (2, 1, 0, 3)).reshape(1, rows, TPF * CELLS, CH)  2.13 us

profile of v1, /device:TPU:0, one launch (start us, length us, event | category | flops | bytes accessed | tf_op | source)
XLA Modules:
  0.0 81.3 jit_solution(18175099040713180492)
XLA Ops:
  1.9 1.5 %copy.17 = f32[1,128,64]{2,1,0:T(8,128)} copy(f32[1,128,64]{1,2,0:T(8,128)} %param.15) | data formatting | bytes 65536 | tf_op args[3]
  3.4 2.2 %copy.18.hw_ref = bf16[3072,64]{1,0:T(8,128)(2,1)} copy(bf16[3072,64]{0,1:T(8,128)(2,1)} %param.16) | data formatting | bytes 786432 | tf_op args[4]
  5.6 72.2 %shard_map.131 = (bf16[128,64]{1,0:T(8,128)(2,1)}, bf16[16,4,16,256]{3,2,1,0:T(8,128)(2,1)}) custom-call(bf16[128,3072]{1,0:T(8,128)(2,1)} %bitcast.13, bf16[128,1024]{1,0:T(8,128)(2,1)} %bitcast.18, bf16[2,128,1024]{2,1,0:T(8,128)(2,1)} %bitcast.14, f32[128,64]{1,0:T(8,128)} %bitcast.17, bf16[3072,64]{1,0:T(8,128)(2,1)} %copy.18.hw_ref, s32[1]{0:T(128)S(6)} %copy.21.ts_ref, ...), custom_call_target="tpu_custom_call" | custom-call | tf_op jit(solution)/shard_map/pallas_call | solution.py:421
  77.7 1.4 %copy.20 = bf16[1,128,64]{1,2,0:T(8,128)(2,1)} copy(bf16[1,128,64]{2,1,0:T(8,128)(2,1)} %bitcast.20) | data formatting | bytes 32768
  79.2 2.1 %copy.19 = bf16[16,4,16,256]{3,2,1,0:T(8,128)(2,1)} copy(bf16[16,4,16,256]{3,0,1,2:T(8,128)(2,1)} %bitcast.16) | data formatting | bytes 1048576 | tf_op jit(solution)/shard_map/transpose | solution.py:487

commit v2 on v1

--- a/solution.py
+++ b/solution.py
@@ -64,9 +64,7 @@
     v_all,
     k_use,
     v_use,
-    w_raw,
-    w_low,
-    w_high,
+    w_use,
     vel_out,
     vel_in,
     win,
@@ -92,7 +90,6 @@
     group = QH // KVH
     slots = kvh_ref.shape[0] + 1
     tokens = q_ref.shape[0]
-    half = tokens // 2
     tile_count = tokens // (TPF * 4)
     rows = n_video * CAP
 
@@ -188,25 +185,22 @@
     for head in range(heads):
         source, place = q_part(me, me, head)
         own.append(pltpu.make_async_copy(source, place, own_sem.at[4 + head]))
-    w_rows = pl.ds(pl.multiple_of(me * heads * HD, HD), heads * HD)
-    own.append(pltpu.make_async_copy(hw_ref.at[w_rows], w_raw, own_sem.at[4 + heads]))
-    own.append(pltpu.make_async_copy(win_ref, win, own_sem.at[5 + heads]))
-    own.append(pltpu.make_async_copy(w2_ref, w2, own_sem.at[6 + heads]))
+    own.append(pltpu.make_async_copy(win_ref, win, own_sem.at[4 + heads]))
+    own.append(pltpu.make_async_copy(w2_ref, w2, own_sem.at[5 + heads]))
+    for head in range(heads):
+        columns = pl.ds(pl.multiple_of((me * heads + head) * HD, HD), HD)
+        own.append(
+            pltpu.make_async_copy(hw_ref.at[:, columns], w_use.at[head], own_sem.at[6 + heads + head])
+        )
     for copy in own:
         copy.start()
-
-    width = w_raw.shape[1]
-    own[4 + heads].wait()
-    shape = (width, 2 * width)
-    w_low[...] = dot(w_raw[...], one_hot(iota(shape, 1) == iota(shape, 0))).astype(BF16)
-    w_high[...] = dot(w_raw[...], one_hot(iota(shape, 1) == iota(shape, 0) + width)).astype(BF16)
 
     def clear(cell, carry):
         toeplitz[cell] = jnp.zeros(toeplitz.shape[1:], BF16)
         return carry
 
     lax.fori_loop(0, CELLS, clear, 0)
-    own[5 + heads].wait()
+    own[4 + heads].wait()
     for y in range(TS):
         for x in range(TS):
             first = max(0, x - 1)
@@ -244,19 +238,16 @@
     ).astype(BF16)
     past_sent = dot(past_match, past_rows)
 
-    shape = (2 * width, WIDE)
+    width = hw_ref.shape[0]
+    shape = (width, WIDE)
     lane = iota(shape, 1)
     cell = lane // LC
-    wanted = (cell // TS % 2 * 2 + cell % 2) * LC + lane % LC
-    spread_low = one_hot(iota(shape, 0) == wanted)
-    spread_high = one_hot(iota(shape, 0) == wanted + width)
+    spread_lanes = one_hot(iota(shape, 0) == (cell // TS % 2 * 2 + cell % 2) * LC + lane % LC)
     shape = (tokens, WIDE)
     cell = iota(shape, 1) // LC
     in_place = iota(shape, 0) % 4 == cell // TS // 2 * 2 + cell % TS // 2
 
-    noisy = noisy_ref[...]
-    noisy = jnp.concatenate([noisy[:half], noisy[half:]], axis=1)
-    fraction = jnp.full((half, 2 * width), ts_ref[0], jnp.int32).astype(F32) / 1000.0
+    fraction = jnp.full((width, tokens), ts_ref[0], jnp.int32).astype(F32) / 1000.0
     step_size = noise_level(fraction - 0.25) - noise_level(fraction)
 
     held = jnp.full((tokens, HD), counts_ref[0], jnp.int32)
@@ -297,21 +288,23 @@
         weights = jnp.exp2((scores - top) * scale).astype(BF16)
         mixed = dot(weights, v_use[...].reshape(key_count, 2 * HD))
         attended = (mixed[:, :HD] / mixed[:, HD:]).astype(BF16)
-        columns = pl.ds(pl.multiple_of(head * HD, HD), HD)
-        return dot(attended[:half], w_low[columns]) + dot(attended[half:], w_high[columns])
+        return lax.dot_general(
+            w_use[head], attended, (((1,), (1,)), ((), ())), preferred_element_type=F32
+        )
 
     for head in range(heads):
         own[4 + head].wait()
-    zero = jnp.zeros((half, 2 * width), F32)
-    vel_in[me] = lax.fori_loop(0, heads, lambda h, total: total + attend(me, h), zero)
-    for k in range(1, n_seq):
+        own[6 + heads + head].wait()
+    zero = jnp.zeros((width, tokens), F32)
+    vel_in[me] = lax.fori_loop(0, heads, lambda h, total: total + attend(me, h), zero, unroll=3)
+    for k in send_order:
         source = seq_peer(k)
 
         def one_head(head, total, source=source):
             q_copy(me, source, head).wait_recv()
             return total + attend(source, head)
 
-        vel_out[source] = lax.fori_loop(0, heads, one_head, zero)
+        vel_out[source] = lax.fori_loop(0, heads, one_head, zero, unroll=3)
         vel_copy(source, me).start()
 
     for k in range(1, n_seq):
@@ -319,9 +312,9 @@
     velocity = vel_in[0]
     for k in range(1, n_seq):
         velocity = velocity + vel_in[k]
-    latent = (noisy + step_size * velocity).astype(BF16)
-
-    spread = jnp.concatenate([dot(latent, spread_low), dot(latent, spread_high)], axis=0)
+    latent = (noisy_ref[...] + step_size * velocity).astype(BF16)
+
+    spread = dot(jnp.transpose(latent.astype(F32)).astype(BF16), spread_lanes)
     spread = jnp.where(in_place, spread, 0.0).astype(BF16)
     tiles_out[...] = (
         (dot(token_match, spread) + past_sent).astype(BF16).reshape(n_video, PACK, WIDE)
@@ -329,8 +322,7 @@
     for k in range(1, n_video):
         tile_copy(video_peer(k), mv).start()
     tiles_in[mv] = tiles_out[mv]
-    nl_ref[:half] = latent[:, :width]
-    nl_ref[half:] = latent[:, width:]
+    nl_ref[...] = latent
 
     shape = ((PAST + FRAMES) * rows, n_video * PACK)
     row = iota(shape, 0)
@@ -339,7 +331,7 @@
     gather = one_hot(
         (iota(shape, 1) == item // CAP * PACK + frame * CAP + item % CAP) & (frame >= 0)
     )
-    own[6 + heads].wait()
+    own[5 + heads].wait()
     for k in range(1, n_video):
         tile_copy(mv, video_peer(k)).wait_recv()
     frames = dot(gather, tiles_in[...].reshape(n_video * PACK, WIDE)).astype(BF16)
@@ -358,7 +350,7 @@
         acc[y, x] = wide[PAST * rows :].reshape(TPF, rows, CH)
         return carry
 
-    lax.fori_loop(0, CELLS, first_conv, 0)
+    lax.fori_loop(0, CELLS, first_conv, 0, unroll=4)
 
     for dy in range(3):
         for dx in range(3):
@@ -421,7 +413,7 @@
     next_latent, decoded = pl.pallas_call(
         functools.partial(step_kernel, n_seq, n_video),
         out_shape=(
-            jax.ShapeDtypeStruct((tokens, width), BF16),
+            jax.ShapeDtypeStruct((width, tokens), BF16),
             jax.ShapeDtypeStruct((CELLS, TPF, rows, CH), BF16),
         ),
         in_specs=[
@@ -445,11 +437,9 @@
             pltpu.VMEM((n_seq, slots, tokens, HD), BF16),
             pltpu.VMEM((n_seq, slots, tokens, HD), BF16),
             pltpu.VMEM((n_seq, slots, tokens, 2 * HD), BF16),
-            pltpu.VMEM((heads * HD, width), BF16),
-            pltpu.VMEM((heads * HD, 2 * width), BF16),
-            pltpu.VMEM((heads * HD, 2 * width), BF16),
-            pltpu.VMEM((n_seq, tokens // 2, 2 * width), F32),
-            pltpu.VMEM((n_seq, tokens // 2, 2 * width), F32),
+            pltpu.VMEM((heads, width, HD), BF16),
+            pltpu.VMEM((n_seq, width, tokens), F32),
+            pltpu.VMEM((n_seq, width, tokens), F32),
             pltpu.VMEM((3, 9 * LC, CH), BF16),
             pltpu.VMEM((3, 9, CH, CH), BF16),
             pltpu.VMEM((CELLS, 3, WIDE, CH), BF16),
@@ -465,7 +455,7 @@
             dma((n_seq,)),
             dma((n_video,)),
             dma((n_video,)),
-            dma((7 + heads,)),
+            dma((6 + 2 * heads,)),
         ],
         compiler_params=pltpu.CompilerParams(
             collective_id=0, has_side_effects=True, vmem_limit_bytes=56 * 1024 * 1024
@@ -474,8 +464,8 @@
         queries[0],
         kv_current[0],
         kv_history[0],
-        noisy_latent[0],
-        head_weight,
+        noisy_latent[0].T,
+        head_weight.T,
         timesteps,
         counts,
         past_latent[0],
@@ -485,7 +475,7 @@
         norm_gain[None],
     )
     decoded = jnp.transpose(decoded, (2, 1, 0, 3)).reshape(1, rows, TPF * CELLS, CH)
-    return next_latent[None], decoded
+    return next_latent.T[None], decoded
 
 
 def solution(mesh):

time: 81.7 us -> 69.8 us (0.85)
  the two profiles are of different devices: /device:TPU:0 before, /device:TPU:17 now
where the time goes in v2:
time: 69.8 us; the launch traced here: 69.5 us
  Pallas kernels  64.1 us (92%)
  local copies, waits for them, and re-layouts  3.45 us (5%)
  between operations  1.93 us (3%)
    pallas_call x1, Pallas kernels, on_device(): pl.pallas_call(functools.partial(step_kernel, n_seq, n_video), out_shape=...  64.1 us
    transpose x1, local copies, waits for them, and re-layouts, on_device(): jnp.transpose(decoded, (2, 1, 0, 3)).reshape(1, rows, TPF * CELLS, CH)  2.13 us

profile of v2, /device:TPU:17, one launch (start us, length us, event | category | flops | bytes accessed | tf_op | source)
XLA Modules:
  0.0 69.5 jit_solution(12782316449359032470)
XLA Ops:
  1.9 64.1 %shard_map.131 = (bf16[64,128]{1,0:T(8,128)(2,1)}, bf16[16,4,16,256]{3,2,1,0:T(8,128)(2,1)}) custom-call(bf16[128,3072]{1,0:T(8,128)(2,1)} %bitcast.18, bf16[128,1024]{1,0:T(8,128)(2,1)} %bitcast.23, bf16[2,128,1024]{2,1,0:T(8,128)(2,1)} %bitcast.21, f32[64,128]{1,0:T(8,128)} %bitcast.25, bf16[64,3072]{1,0:T(8,128)(2,1)} %bitcast.22, s32[1]{0:T(128)S(6)} %copy.16.ts_ref, ...), custom_call_target="tpu_custom_call" | custom-call | tf_op jit(solution)/shard_map/pallas_call | solution.py:413
  66.0 2.1 %copy.14 = bf16[16,4,16,256]{3,2,1,0:T(8,128)(2,1)} copy(bf16[16,4,16,256]{3,0,1,2:T(8,128)(2,1)} %bitcast.20) | data formatting | bytes 1048576 | tf_op jit(solution)/shard_map/transpose | solution.py:477
  68.2 1.3 %copy.18 = bf16[1,128,64]{1,2,0:T(8,128)(2,1)} copy(bf16[1,128,64]{1,2,0:T(8,128)(2,1)} %bitcast.26) | data formatting | bytes 32768

commit v3 on v2

--- a/solution.py
+++ b/solution.py
@@ -170,14 +170,23 @@
         for part in range(4):
             kv_copy(seq_peer(k), me, part).start()
 
-    for k in send_order:
-        target = seq_peer(k)
-
-        def send_head(head, carry, target=target):
-            q_copy(target, me, head).start()
+    def kv_sent(k):
+        for part in range(4):
+            kv_copy(seq_peer(k), me, part).wait_send()
+
+    def send_heads(k, first, last):
+        def one(head, carry):
+            q_copy(seq_peer(k), me, head).start()
             return carry
 
-        lax.fori_loop(0, heads, send_head, 0)
+        lax.fori_loop(first, last, one, 0)
+
+    def heads_sent(k, first, last):
+        def one(head, carry):
+            q_copy(seq_peer(k), me, head).wait_send()
+            return carry
+
+        lax.fori_loop(first, last, one, 0)
 
     own = []
     for part, (source, place) in enumerate(kv_parts(me, me)):
@@ -267,6 +276,12 @@
             ).astype(BF16)
             v_use[source, slot, :, HD:] = jnp.where(valid, 1.0, 0.0).astype(BF16)
 
+    kv_sent(1)
+    send_heads(1, 0, heads)
+    for k in range(n_seq - 1, 1, -1):
+        kv_sent(k)
+        if k == n_seq - 1:
+            send_heads(k, 0, heads)
     for part in range(4):
         own[part].wait()
     take_rows(me)
@@ -297,7 +312,10 @@
         own[6 + heads + head].wait()
     zero = jnp.zeros((width, tokens), F32)
     vel_in[me] = lax.fori_loop(0, heads, lambda h, total: total + attend(me, h), zero, unroll=3)
-    for k in send_order:
+    for k in (1, *range(n_seq - 1, 1, -1)):
+        if k > 2:
+            heads_sent(k, 0, heads)
+            send_heads(k - 1, 0, heads)
         source = seq_peer(k)
 
         def one_head(head, total, source=source):
@@ -371,16 +389,9 @@
     dec_ref[...] = acc[...].reshape(CELLS, TPF, rows, CH).astype(BF16)
 
     for k in range(1, n_seq):
-        target = seq_peer(k)
-        for part in range(4):
-            kv_copy(target, me, part).wait_send()
-
-        def sent_head(head, carry, target=target):
-            q_copy(target, me, head).wait_send()
-            return carry
-
-        lax.fori_loop(0, heads, sent_head, 0)
-        vel_copy(target, me).wait_send()
+        if k == 1 or k == 2:
+            heads_sent(k, 0, heads)
+        vel_copy(seq_peer(k), me).wait_send()
     for k in range(1, n_video):
         tile_copy(video_peer(k), mv).wait_send()
 

time: 69.8 us -> 64.1 us (0.918)
  the two profiles are of different devices: /device:TPU:17 before, /device:TPU:9 now
where the time goes in v3:
time: 64.1 us; the launch traced here: 63.8 us
  Pallas kernels  58.4 us (91%)
  local copies, waits for them, and re-layouts  3.45 us (5%)
  between operations  1.93 us (3%)
    pallas_call x1, Pallas kernels, on_device(): pl.pallas_call(functools.partial(step_kernel, n_seq, n_video), out_shape=...  58.4 us
    transpose x1, local copies, waits for them, and re-layouts, on_device(): jnp.transpose(decoded, (2, 1, 0, 3)).reshape(1, rows, TPF * CELLS, CH)  2.13 us
    unnamed x1, local copies, waits for them, and re-layouts  1.32 us

profile of v3, /device:TPU:9, one launch (start us, length us, event | category | flops | bytes accessed | tf_op | source)
XLA Modules:
  0.0 63.8 jit_solution(3643271625056189342)
XLA Ops:
  1.9 58.4 %shard_map.131 = (bf16[64,128]{1,0:T(8,128)(2,1)}, bf16[16,4,16,256]{3,2,1,0:T(8,128)(2,1)}) custom-call(bf16[128,3072]{1,0:T(8,128)(2,1)} %bitcast.18, bf16[128,1024]{1,0:T(8,128)(2,1)} %bitcast.23, bf16[2,128,1024]{2,1,0:T(8,128)(2,1)} %bitcast.21, f32[64,128]{1,0:T(8,128)} %bitcast.25, bf16[64,3072]{1,0:T(8,128)(2,1)} %bitcast.22, s32[1]{0:T(128)S(6)} %copy.16.ts_ref, ...), custom_call_target="tpu_custom_call" | custom-call | tf_op jit(solution)/shard_map/pallas_call | solution.py:424
  60.3 2.1 %copy.14 = bf16[16,4,16,256]{3,2,1,0:T(8,128)(2,1)} copy(bf16[16,4,16,256]{3,0,1,2:T(8,128)(2,1)} %bitcast.20) | data formatting | bytes 1048576 | tf_op jit(solution)/shard_map/transpose | solution.py:488
  62.4 1.3 %copy.18 = bf16[1,128,64]{1,2,0:T(8,128)(2,1)} copy(bf16[1,128,64]{1,2,0:T(8,128)(2,1)} %bitcast.26) | data formatting | bytes 32768
